TPU v7x, 32 devices: a whole 2x2x4 slice. The times are simulated.
32 devices in a mesh: section: 8 (over z, core), tensor: 4 (over y, x).
Axes of the slice: x: 2, y: 2, z: 4, core: 2. Of those that a mesh axis runs over, the one named last changes fastest.
Arguments:
- value_half: bfloat16 [8, 1024, 8192], P('section', None, 'tensor'), may hold values from -0.125 to 0.125
- out_half: bfloat16 [8, 8192, 1024], P('section', 'tensor'), may hold values from -0.0625 to 0.0625
- saved: bfloat16 [8, 2, 128, 2048], P('section', None, None, 'tensor'), may hold values from -6 to 6
- first_grad: bfloat16 [8, 128, 2048], P('section', None, 'tensor'), may hold values from -6 to 6
- head_grad: bfloat16 [2, 128, 2048], P(None, None, 'tensor'), may hold values from -6 to 6
Outputs:
- sent_grad: bfloat16 [8, 128, 2048], P('section', None, 'tensor')
- value_grad: bfloat16 [8, 1024, 8192], P('section', None, 'tensor')
- out_grad: bfloat16 [8, 8192, 1024], P('section', 'tensor')
All inputs are finite; a program needn't handle non-finite values.
Results may differ from a plain program's by a relative error of at most 0.012.
Values may be sent and summed in bfloat16 or wider, within the bound.
A program may use at most 192 MiB of HBM per device.

v0:
```python
import jax
import jax.numpy as jnp
from jax import lax
from jax.sharding import PartitionSpec as P


def from_behind(block, axis, distance):
    devices = range(lax.axis_size(axis))
    route = [(i - distance, i) for i in devices if i - distance in devices]
    return lax.ppermute(block, axis, route)


def contract_last(left, right):
    return lax.dot_general(
        left, right, (((1,), (1,)), ((), ())), preferred_element_type=jnp.float32
    )


def contract_first(left, right):
    return lax.dot_general(
        left, right, (((0,), (0,)), ((), ())), preferred_element_type=jnp.float32
    )


def block_backward(inputs, incoming, w_value, w_out):
    preact = jnp.dot(inputs, w_value, preferred_element_type=jnp.float32)
    sigmoid_val = jax.nn.sigmoid(preact)
    activation = (preact * sigmoid_val).astype(jnp.bfloat16)
    slope = sigmoid_val * (1.0 + preact * (1.0 - sigmoid_val))
    gathered = lax.all_gather(incoming, "tensor", axis=1, tiled=True)
    backgrad = contract_last(gathered, w_out)
    grad_pre = (backgrad * slope).astype(jnp.bfloat16)
    partial_value = contract_last(grad_pre, w_value)
    summed = lax.psum_scatter(
        partial_value.astype(jnp.bfloat16), "tensor", scatter_dimension=1, tiled=True
    ).astype(jnp.float32)
    passed = (incoming.astype(jnp.float32) + summed).astype(jnp.bfloat16)
    return (passed, grad_pre, activation, gathered)


def body(value_half, out_half, saved, first_grad, head_grad):
    section_count = lax.axis_size("section")
    half_count = section_count // 2
    position = lax.axis_index("section")
    copy_bit = position // half_count
    is_lower = copy_bit == 0
    value_mine = value_half[0]
    out_mine = out_half[0]
    half_rows = value_mine.shape[0]
    inner_width = value_mine.shape[1]
    flattened = (value_mine.reshape(section_count, -1), out_mine.reshape(section_count, -1))
    spread_parts = (
        lax.all_to_all(flattened[0], "section", split_axis=0, concat_axis=0, tiled=True),
        lax.all_to_all(flattened[1], "section", split_axis=0, concat_axis=0, tiled=True),
    )
    rolled_parts = (
        jnp.roll(spread_parts[0], -half_count, 0),
        jnp.roll(spread_parts[1], -half_count, 0),
    )
    routed_parts = (
        lax.all_to_all(rolled_parts[0], "section", split_axis=0, concat_axis=0, tiled=True),
        lax.all_to_all(rolled_parts[1], "section", split_axis=0, concat_axis=0, tiled=True),
    )
    value_other = routed_parts[0].reshape(half_rows, inner_width)
    out_other = routed_parts[1].reshape(inner_width, half_rows)
    value_top = jnp.where(is_lower, value_mine, value_other)
    value_bottom = jnp.where(is_lower, value_other, value_mine)
    out_left = jnp.where(is_lower, out_mine, out_other)
    out_right = jnp.where(is_lower, out_other, out_mine)
    w_value = jnp.concatenate([value_top, value_bottom], 0)
    w_out = jnp.concatenate([out_left, out_right], 1)
    whole_inputs = lax.all_gather(saved[0], "tensor", axis=2, tiled=True)
    passed_first, pre_first, act_first, grad_first = block_backward(
        whole_inputs[0], first_grad[0], w_value, w_out
    )
    from_next = from_behind(passed_first, "section", -1)
    at_end = position % half_count == half_count - 1
    head_mine = jnp.where(is_lower, head_grad[0], head_grad[1])
    incoming = jnp.where(at_end, head_mine, from_next)
    passed_second, pre_second, act_second, grad_second = block_backward(
        whole_inputs[1], incoming, w_value, w_out
    )
    both_inputs = whole_inputs.reshape(-1, whole_inputs.shape[2])
    both_pre = jnp.concatenate([pre_first, pre_second], 0)
    both_act = jnp.concatenate([act_first, act_second], 0)
    both_grad = jnp.concatenate([grad_first, grad_second], 0)
    value_total = contract_first(both_inputs, both_pre).astype(jnp.bfloat16)
    out_total = contract_first(both_act, both_grad).astype(jnp.bfloat16)
    give_offset = (1 - copy_bit) * half_rows
    keep_offset = copy_bit * half_rows
    give_value = lax.dynamic_slice_in_dim(value_total, give_offset, half_rows, 0)
    give_out = lax.dynamic_slice_in_dim(out_total, give_offset, half_rows, 1)
    outgoing = (give_value.reshape(section_count, -1), give_out.reshape(section_count, -1))
    grad_spread_parts = (
        lax.all_to_all(outgoing[0], "section", split_axis=0, concat_axis=0, tiled=True),
        lax.all_to_all(outgoing[1], "section", split_axis=0, concat_axis=0, tiled=True),
    )
    grad_rolled = (
        jnp.roll(grad_spread_parts[0], -half_count, 0),
        jnp.roll(grad_spread_parts[1], -half_count, 0),
    )
    grad_routed = (
        lax.all_to_all(grad_rolled[0], "section", split_axis=0, concat_axis=0, tiled=True),
        lax.all_to_all(grad_rolled[1], "section", split_axis=0, concat_axis=0, tiled=True),
    )
    keep_value = lax.dynamic_slice_in_dim(value_total, keep_offset, half_rows, 0)
    keep_out = lax.dynamic_slice_in_dim(out_total, keep_offset, half_rows, 1)
    value_grad = (
        keep_value.astype(jnp.float32)
        + grad_routed[0].reshape(half_rows, inner_width).astype(jnp.float32)
    ).astype(jnp.bfloat16)
    out_grad = (
        keep_out.astype(jnp.float32)
        + grad_routed[1].reshape(inner_width, half_rows).astype(jnp.float32)
    ).astype(jnp.bfloat16)
    return (passed_second[None], value_grad[None], out_grad[None])


def solution(mesh):
    return jax.shard_map(
        body,
        mesh=mesh,
        in_specs=(
            P("section", None, "tensor"),
            P("section", "tensor", None),
            P("section", None, None, "tensor"),
            P("section", None, "tensor"),
            P(None, None, "tensor"),
        ),
        out_specs=(
            P("section", None, "tensor"),
            P("section", None, "tensor"),
            P("section", "tensor", None),
        ),
        check_vma=False,
    )
```

profile of v0, /device:TPU:0, one launch (start us, length us, event | category | flops | bytes accessed | tf_op | source)
XLA Modules:
  0.0 1085.3 jit_solution(8713891806258183700)
XLA Ops:
  7.2 8.5 all_to_all.64
  16.2 27.2 %reduce.6 = bf16[8,262144]{1,0:T(8,128)(2,1)} reduce(bf16[8,1,262144]{2,1,0:T(2,128)(2,1)} %all_to_all.64, bf16[]{:T(256)} %broadcast.16), dimensions={1}, to_apply=%all_to_all.64.reduce_sub_computation | reduce | bytes 8388610 | tf_op jit(solution)/shard_map/all_to_all | solution.py:54
  43.4 8.1 reshape.74
  51.5 6.6 all-to-all-start
  58.1 10.4 all_to_all.65
  68.5 27.2 %reduce.8 = bf16[8,262144]{1,0:T(8,128)(2,1)} reduce(bf16[8,1,262144]{2,1,0:T(2,128)(2,1)} %all_to_all.65, bf16[]{:T(256)} %broadcast.16), dimensions={1}, to_apply=%all_to_all.65.reduce_sub_computation | reduce | bytes 8388610 | tf_op jit(solution)/shard_map/all_to_all | solution.py:53
  95.6 8.0 reshape.78
  103.7 48.4 %all-to-all-done = bf16[8,2,131072]{2,1,0:T(2,128)(2,1)} async-done(((bf16[8,2,131072]{2,1,0:T(2,128)(2,1)}), bf16[8,2,131072]{2,1,0:T(2,128)(2,1)}, u32[]{:S(2)}, u32[]{:S(2)}) %all-to-all-start) | async-done | bytes 4194336 | tf_op jit(solution)/shard_map/all_to_all | solution.py:54
  152.1 5.0 all-to-all-start.2
  157.1 8.8 reshape.75
  165.9 10.0 fusion.29
  175.9 5.2 copy_bitcast_fusion.3
  184.5 6.3 reduce.7
  190.8 8.1 reshape.76
  198.9 52.2 %all-to-all-done.2 = bf16[8,2,131072]{2,1,0:T(2,128)(2,1)} async-done(((bf16[8,2,131072]{2,1,0:T(2,128)(2,1)}), bf16[8,2,131072]{2,1,0:T(2,128)(2,1)}, u32[]{:S(2)}, u32[]{:S(2)}) %all-to-all-start.2) | async-done | bytes 4194336 | tf_op jit(solution)/shard_map/all_to_all | solution.py:53
  255.9 8.8 reshape.79
  264.7 10.0 fusion.28
  274.7 5.2 copy_bitcast_fusion.2
  283.3 6.2 reduce.9
  289.5 8.0 reshape.80
  297.6 52.3 %all-to-all-done.1 = bf16[8,2,131072]{2,1,0:T(2,128)(2,1)} async-done(((bf16[8,2,131072]{2,1,0:T(2,128)(2,1)}), bf16[8,2,131072]{2,1,0:T(2,128)(2,1)}, u32[]{:S(2)}, u32[]{:S(2)}) %all-to-all-start.1) | async-done | bytes 4194336 | tf_op jit(solution)/shard_map/all_to_all | solution.py:62
  355.3 10.9 %all-gather = bf16[1,128,2048]{2,1,0:T(8,128)(2,1)S(1)} all-gather(bf16[1,128,512]{2,1,0:T(8,128)(2,1)S(1)} %copy-done.11), channel_id=2, replica_groups=mesh['section'=8,'tensor'=4] {'tensor'}, dimensions={2}, use_global_device_ids=true | all-gather | bytes 655360 | tf_op jit(solution)/shard_map/all_gather | solution.py:30
  366.2 8.8 reshape.77
  375.0 26.5 %reduce = bf16[8,262144]{1,0:T(8,128)(2,1)} reduce(bf16[8,1,262144]{2,1,0:T(2,128)(2,1)} %reshape.77, bf16[]{:T(256)} %constant.45), dimensions={1}, to_apply=%all_to_all.51.reduce_sub_computation | reduce | bytes 8388610 | tf_op jit(solution)/shard_map/all_to_all | solution.py:62
  401.5 6.1 reshape.57
  407.6 40.8 %all-to-all-done.3 = bf16[8,2,131072]{2,1,0:T(2,128)(2,1)} async-done(((bf16[8,2,131072]{2,1,0:T(2,128)(2,1)}), bf16[8,2,131072]{2,1,0:T(2,128)(2,1)}, u32[]{:S(2)}, u32[]{:S(2)}) %all-to-all-start.3) | async-done | bytes 4194336 | tf_op jit(solution)/shard_map/all_to_all | solution.py:61
  448.5 8.8 reshape.81
  457.2 26.5 %reduce.1 = bf16[8,262144]{1,0:T(8,128)(2,1)} reduce(bf16[8,1,262144]{2,1,0:T(2,128)(2,1)} %reshape.81, bf16[]{:T(256)} %constant.45), dimensions={1}, to_apply=%all_to_all.55.reduce_sub_computation | reduce | bytes 8388610 | tf_op jit(solution)/shard_map/all_to_all | solution.py:61
  483.8 6.0 reshape.58
  489.8 6.8 bitcast_select_fusion.3
  515.4 23.8 %reduce-scatter.3.cloned.1.call-done = bf16[128,512]{1,0:T(8,128)(2,1)} async-done(((bf16[128,2048]{1,0:T(8,128)(2,1)}), bf16[128,512]{1,0:T(8,128)(2,1)}) %reduce-scatter.3.cloned.1.call-update) | async-done | bytes 131088 | tf_op jit(solution)/shard_map/reduce_scatter | solution.py:34
  541.7 5.0 multiply_convert_fusion
  546.8 10.7 all_gather.11
  569.2 6.4 copy.31
  575.6 10.4 all_to_all.66
  586.0 27.2 %reduce.10 = bf16[8,262144]{1,0:T(8,128)(2,1)} reduce(bf16[8,1,262144]{2,1,0:T(2,128)(2,1)} %all_to_all.66, bf16[]{:T(256)} %broadcast.16), dimensions={1}, to_apply=%all_to_all.66.reduce_sub_computation | reduce | bytes 8388610 | tf_op jit(solution)/shard_map/all_to_all | solution.py:95
  613.1 8.1 reshape.82
  634.3 8.5 all_to_all.67
  642.8 27.2 %reduce.12 = bf16[8,262144]{1,0:T(8,128)(2,1)} reduce(bf16[8,1,262144]{2,1,0:T(2,128)(2,1)} %all_to_all.67, bf16[]{:T(256)} %broadcast.16), dimensions={1}, to_apply=%all_to_all.67.reduce_sub_computation | reduce | bytes 8388610 | tf_op jit(solution)/shard_map/all_to_all | solution.py:96
  670.0 8.0 reshape.86
  678.1 42.0 %all-to-all-done.4 = bf16[8,2,131072]{2,1,0:T(2,128)(2,1)} async-done(((bf16[8,2,131072]{2,1,0:T(2,128)(2,1)}), bf16[8,2,131072]{2,1,0:T(2,128)(2,1)}, u32[]{:S(2)}, u32[]{:S(2)}) %all-to-all-start.4) | async-done | bytes 4194336 | tf_op jit(solution)/shard_map/all_to_all | solution.py:95
  720.0 5.0 all-to-all-start.6
  725.0 8.8 reshape.83
  733.8 10.0 fusion.27
  756.0 6.5 reduce.11
  762.5 8.1 reshape.84
  770.6 48.4 %all-to-all-done.6 = bf16[8,2,131072]{2,1,0:T(2,128)(2,1)} async-done(((bf16[8,2,131072]{2,1,0:T(2,128)(2,1)}), bf16[8,2,131072]{2,1,0:T(2,128)(2,1)}, u32[]{:S(2)}, u32[]{:S(2)}) %all-to-all-start.6) | async-done | bytes 4194336 | tf_op jit(solution)/shard_map/all_to_all | solution.py:96
  823.6 8.8 reshape.87
  832.4 10.0 fusion.26
  854.6 6.6 reduce.13
  861.1 8.0 reshape.88
  869.2 48.4 %all-to-all-done.5 = bf16[8,2,131072]{2,1,0:T(2,128)(2,1)} async-done(((bf16[8,2,131072]{2,1,0:T(2,128)(2,1)}), bf16[8,2,131072]{2,1,0:T(2,128)(2,1)}, u32[]{:S(2)}, u32[]{:S(2)}) %all-to-all-start.5) | async-done | bytes 4194336 | tf_op jit(solution)/shard_map/all_to_all | solution.py:103
  922.2 6.1 convolution_convert_fusion.2
  928.4 25.3 %reduce-scatter.5.cloned.1.call-done = bf16[128,512]{1,0:T(8,128)(2,1)} async-done(((bf16[128,2048]{1,0:T(8,128)(2,1)}), bf16[128,512]{1,0:T(8,128)(2,1)}) %reduce-scatter.5.cloned.1.call-update) | async-done | bytes 131088 | tf_op jit(solution)/shard_map/reduce_scatter | solution.py:34
  955.3 8.8 reshape.85
  964.0 28.5 %convert_reduce_fusion.1 = f32[8,262144]{1,0:T(8,128)} fusion(bf16[8,1,262144]{2,1,0:T(2,128)(2,1)} %reshape.85), kind=kLoop, calls=%fused_computation.5 | loop fusion | flops 2097152 | bytes 12582912 | tf_op jit(solution)/shard_map/convert_element_type | solution.py:110
  992.5 8.1 reshape.60
  1000.6 9.2 copy.35
  1009.9 8.2 fusion.4
  1018.1 6.4 copy.39
  1024.5 8.8 reshape.89
  1033.3 28.8 %convert_reduce_fusion = f32[8,262144]{1,0:T(8,128)} fusion(bf16[8,1,262144]{2,1,0:T(2,128)(2,1)} %reshape.89), kind=kLoop, calls=%fused_computation.4 | loop fusion | flops 2097152 | bytes 12582912 | tf_op jit(solution)/shard_map/convert_element_type | solution.py:114
  1062.1 8.1 reshape.61
  1070.2 8.2 fusion.3
  (70 shorter events, 98.3 us)
Async XLA Ops:
  51.5 100.6 %all-to-all-start = ((bf16[8,2,131072]{2,1,0:T(2,128)(2,1)}), bf16[8,2,131072]{2,1,0:T(2,128)(2,1)}, u32[]{:S(2)}, u32[]{:S(2)}) async-start(bf16[8,2,131072]{2,1,0:T(2,128)(2,1)} %reshape.74), calls=%async_computation | async-start | bytes 8388608 | tf_op jit(solution)/shard_map/all_to_all | solution.py:54
  152.1 99.0 %all-to-all-start.2 = ((bf16[8,2,131072]{2,1,0:T(2,128)(2,1)}), bf16[8,2,131072]{2,1,0:T(2,128)(2,1)}, u32[]{:S(2)}, u32[]{:S(2)}) async-start(bf16[8,2,131072]{2,1,0:T(2,128)(2,1)} %reshape.78), calls=%async_computation.2 | async-start | bytes 8388608 | tf_op jit(solution)/shard_map/all_to_all | solution.py:53
  251.1 98.8 %all-to-all-start.1 = ((bf16[8,2,131072]{2,1,0:T(2,128)(2,1)}), bf16[8,2,131072]{2,1,0:T(2,128)(2,1)}, u32[]{:S(2)}, u32[]{:S(2)}) async-start(bf16[8,2,131072]{2,1,0:T(2,128)(2,1)} %reshape.76), calls=%async_computation.1 | async-start | bytes 8388608 | tf_op jit(solution)/shard_map/all_to_all | solution.py:62
  297.6 57.7 %copy-start.11 = (bf16[1,128,512]{2,1,0:T(8,128)(2,1)S(1)}, bf16[1,128,512]{2,1,0:T(8,128)(2,1)}, u32[]{:S(2)}) copy-start(bf16[1,128,512]{2,1,0:T(8,128)(2,1)} %param.8) | copy-start | bytes 393220
  349.9 98.6 %all-to-all-start.3 = ((bf16[8,2,131072]{2,1,0:T(2,128)(2,1)}), bf16[8,2,131072]{2,1,0:T(2,128)(2,1)}, u32[]{:S(2)}, u32[]{:S(2)}) async-start(bf16[8,2,131072]{2,1,0:T(2,128)(2,1)} %reshape.80), calls=%async_computation.3 | async-start | bytes 8388608 | tf_op jit(solution)/shard_map/all_to_all | solution.py:61
  354.5 147.6 %all-gather.4.cloned.1.call-start = ((), (), s32[]{:S(2)}) async-start(), calls=%async_computation.12 | async-start | bytes 1310720 | tf_op jit(solution)/shard_map/all_gather | solution.py:72
  355.2 184.0 %reduce-scatter.3.cloned.1.call-start = ((), (), s32[]{:S(2)}) async-start(), calls=%async_computation.10 | async-start | bytes 655360 | tf_op jit(solution)/shard_map/reduce_scatter | solution.py:34
  489.8 7.2 copy-start.2
  489.8 8.8 copy-start.3
  502.1 4.8 copy-start.6
  502.1 6.1 copy-start.8
  508.2 3.3 copy-start.4
  508.2 3.5 copy-start.5
  511.7 3.7 copy-start.14
  511.7 30.1 %copy-start.10 = (bf16[1,2,128,2048]{3,2,1,0:T(8,128)(2,1)S(1)}, bf16[1,2,128,2048]{3,2,1,0:T(8,128)(2,1)}, u32[]{:S(2)}) copy-start(bf16[1,2,128,2048]{3,2,1,0:T(8,128)(2,1)} %all-gather.4.cloned.1.call-done) | copy-start | bytes 3145732
  540.1 6.6 copy-start.16
  540.1 17.4 %copy-start.7 = (bf16[2048,1024]{1,0:T(8,128)(2,1)S(1)}, bf16[2048,1024]{1,0:T(8,128)(2,1)}, u32[]{:S(2)}) copy-start(bf16[2048,1024]{1,0:T(8,128)(2,1)} %get-tuple-element.23) | copy-start | bytes 12582916
  540.2 17.4 %copy-start.9 = (bf16[2048,1024]{1,0:T(8,128)(2,1)S(1)}, bf16[2048,1024]{1,0:T(8,128)(2,1)}, u32[]{:S(2)}) copy-start(bf16[2048,1024]{1,0:T(8,128)(2,1)} %get-tuple-element.24) | copy-start | bytes 12582916
  540.2 6.6 collective-permute-start
  557.5 3.3 copy-start.15
  560.8 2.4 copy-start.12
  563.3 3.2 copy-start
  621.2 98.8 %all-to-all-start.4 = ((bf16[8,2,131072]{2,1,0:T(2,128)(2,1)}), bf16[8,2,131072]{2,1,0:T(2,128)(2,1)}, u32[]{:S(2)}, u32[]{:S(2)}) async-start(bf16[8,2,131072]{2,1,0:T(2,128)(2,1)} %reshape.82), calls=%async_computation.6 | async-start | bytes 8388608 | tf_op jit(solution)/shard_map/all_to_all | solution.py:95
  628.4 3.2 copy-start.1
  720.0 99.0 %all-to-all-start.6 = ((bf16[8,2,131072]{2,1,0:T(2,128)(2,1)}), bf16[8,2,131072]{2,1,0:T(2,128)(2,1)}, u32[]{:S(2)}, u32[]{:S(2)}) async-start(bf16[8,2,131072]{2,1,0:T(2,128)(2,1)} %reshape.86), calls=%async_computation.8 | async-start | bytes 8388608 | tf_op jit(solution)/shard_map/all_to_all | solution.py:96
  819.0 98.6 %all-to-all-start.5 = ((bf16[8,2,131072]{2,1,0:T(2,128)(2,1)}), bf16[8,2,131072]{2,1,0:T(2,128)(2,1)}, u32[]{:S(2)}, u32[]{:S(2)}) async-start(bf16[8,2,131072]{2,1,0:T(2,128)(2,1)} %reshape.84), calls=%async_computation.7 | async-start | bytes 8388608 | tf_op jit(solution)/shard_map/all_to_all | solution.py:103
  869.2 53.0 %copy-start.13 = (bf16[128,2048]{1,0:T(8,128)(2,1)S(1)}, bf16[128,2048]{1,0:T(8,128)(2,1)}, u32[]{:S(2)}) copy-start(bf16[128,2048]{1,0:T(8,128)(2,1)} %copy-done.12) | copy-start | bytes 1572868
  917.6 106.9 %all-to-all-start.7 = ((bf16[8,2,131072]{2,1,0:T(2,128)(2,1)}), bf16[8,2,131072]{2,1,0:T(2,128)(2,1)}, u32[]{:S(2)}, u32[]{:S(2)}) async-start(bf16[8,2,131072]{2,1,0:T(2,128)(2,1)} %reshape.88), calls=%async_computation.9 | async-start | bytes 8388608 | tf_op jit(solution)/shard_map/all_to_all | solution.py:104
  922.2 31.5 %reduce-scatter.5.cloned.1.call-start = ((), (), s32[]{:S(2)}) async-start(), calls=%async_computation.11 | async-start | bytes 655360 | tf_op jit(solution)/shard_map/reduce_scatter | solution.py:34
Sparse Core Ops, SparseCore 0:
  357.1 27.8 all-gather.3
  515.5 23.6 reduce-scatter.2
  928.5 25.1 reduce-scatter.4
where the time goes:
time: 1090 us
  waiting for transfers between devices  382 us (35%)
  local copies, waits for them, and re-layouts  307 us (28%)
  other arithmetic  287 us (26%)
  starting transfers between devices  41.5 us (4%)
  matrix products  30.7 us (3%)
  blocking collectives  21.7 us (2%)
  between operations  14.6 us (1%)
    unnamed x55, local copies, waits for them, and re-layouts  169 us
    all_to_all x1, waiting for transfers between devices, body(): lax.all_to_all(rolled_parts[1], 'section', split_axis=0, concat_axis=0, t...  52.3 us
    all_to_all x1, waiting for transfers between devices, body(): lax.all_to_all(flattened[0], 'section', split_axis=0, concat_axis=0, tile...  52.2 us
    reduce_scatter x2, waiting for transfers between devices, block_backward(): lax.psum_scatter(partial_value.astype(jnp.bfloat16), 'tensor', scatter_di...  49.1 us
    all_to_all x1, waiting for transfers between devices, body(): lax.all_to_all(flattened[1], 'section', split_axis=0, concat_axis=0, tile...  48.4 us
    all_to_all x1, waiting for transfers between devices, body(): lax.all_to_all(outgoing[1], 'section', split_axis=0, concat_axis=0, tiled...  48.4 us
    all_to_all x1, waiting for transfers between devices, body(): lax.all_to_all(grad_rolled[0], 'section', split_axis=0, concat_axis=0, ti...  48.4 us
    all_to_all x1, waiting for transfers between devices, body(): lax.all_to_all(outgoing[0], 'section', split_axis=0, concat_axis=0, tiled...  42 us
  transfers between devices with their start and end apart: 12, of which 9 were waited for; matrix products, arithmetic and copies ran while one was open for 39% of the time, Pallas kernels for 0%

commit v1 on v0

v1 whole, which is shorter than its diff:
```python
import jax
import jax.numpy as jnp
from jax import lax
from jax.sharding import PartitionSpec as P

F32 = jnp.float32
BF16 = jnp.bfloat16


def dot(left, right, left_dim, right_dim):
    return lax.dot_general(
        left, right, (((left_dim,), (right_dim,)), ((), ())), preferred_element_type=F32
    )


def split_copies(gathered):
    half = gathered.shape[1] // 2
    return jnp.concatenate([gathered[:, :half], gathered[:, half:]], 0)


def body(value_half, out_half, saved, first_grad, head_grad):
    sections = lax.axis_size("section")
    tensors = lax.axis_size("tensor")
    copies = sections // 2
    low = tensors // 2
    position = lax.axis_index("section")
    is_lower = position < copies
    w_value, w_out = value_half[0], out_half[0]
    tok = first_grad.shape[1]

    swap_route = []
    for r in range(sections):
        for t in range(tensors):
            c, s, h, i = r // copies, r % copies, t // low, t % low
            swap_route.append((r * tensors + t, (h * copies + s) * tensors + c * low + i))
    mirror_route = [(r, (r + copies) % sections) for r in range(sections)]
    relay_route = [(r, r - 1) for r in range(1, sections)]

    def swap(block):
        return lax.ppermute(block, ("section", "tensor"), swap_route)

    def mirror(block):
        return lax.ppermute(block, "section", mirror_route)

    def both(partial):
        return partial.astype(F32) + mirror(partial).astype(F32)

    head_mine = jnp.where(is_lower, head_grad[0], head_grad[1])
    mine = jnp.concatenate([first_grad[0], saved[0, 0], saved[0, 1], head_mine], 0)
    swapped = swap(mine)
    first_swapped, head_swapped = swapped[:tok], swapped[3 * tok :]
    gathered = lax.all_gather(swapped[: 3 * tok], "tensor", axis=1, tiled=True)
    grad0 = split_copies(gathered[:tok])
    in0 = split_copies(gathered[tok : 2 * tok])
    in1 = split_copies(gathered[2 * tok :])

    def block(preact, backgrad):
        sigmoid = jax.nn.sigmoid(preact)
        act = (preact * sigmoid).astype(BF16)
        slope = sigmoid * (1.0 + preact * (1.0 - sigmoid))
        return act, (backgrad * slope).astype(BF16)

    def pass_down(pre_grad, incoming):
        partial = dot(pre_grad, w_value, 1, 1).astype(BF16)
        partial = jnp.concatenate([partial[:tok], partial[tok:]], 1)
        summed = lax.psum_scatter(partial, "tensor", scatter_dimension=1, tiled=True)
        return (incoming.astype(F32) + summed.astype(F32)).astype(BF16)

    back0 = both(dot(grad0, w_out, 1, 1).astype(BF16))
    pre0 = both(dot(in0, w_value, 1, 0).astype(BF16))
    act0, e0 = block(pre0, back0)
    pre1 = both(dot(in1, w_value, 1, 0).astype(BF16))
    passed0 = pass_down(e0, first_swapped)
    from_next = lax.ppermute(passed0, "section", relay_route)
    at_end = position % copies == copies - 1
    incoming = jnp.where(at_end, head_swapped, from_next)
    grad1 = split_copies(lax.all_gather(incoming, "tensor", axis=1, tiled=True))
    back1 = both(dot(grad1, w_out, 1, 1).astype(BF16))
    act1, e1 = block(pre1, back1)
    sent = swap(pass_down(e1, incoming))

    inputs = jnp.concatenate([in0, in1], 0)
    grads = jnp.concatenate([grad0, grad1], 0)
    value_grad = dot(inputs, jnp.concatenate([e0, e1], 0), 0, 0).astype(BF16)
    out_grad = dot(jnp.concatenate([act0, act1], 0), grads, 0, 0).astype(BF16)
    return sent[None], value_grad[None], out_grad[None]


def solution(mesh):
    return jax.shard_map(
        body,
        mesh=mesh,
        in_specs=(
            P("section", None, "tensor"),
            P("section", "tensor", None),
            P("section", None, None, "tensor"),
            P("section", None, "tensor"),
            P(None, None, "tensor"),
        ),
        out_specs=(
            P("section", None, "tensor"),
            P("section", None, "tensor"),
            P("section", "tensor", None),
        ),
        check_vma=False,
    )
```

time: 1090 us -> 348 us (0.32)
  local copies, waits for them, and re-layouts: 307 us -> 4.09 us
  other arithmetic: 287 us -> 8.85 us
  waiting for transfers between devices: 382 us -> 272 us
  starting transfers between devices: 41.5 us -> 9.96 us
  blocking collectives: 21.7 us -> 10.2 us
    all_to_all x8 -> x0, waiting for transfers between devices: 333 us -> none  [the longest x1 52.3 us: body(): lax.all_to_all(rolled_parts[1], 'section', split_axis=0, concat_axis=0, t...]
    all_to_all x14 -> x0, other arithmetic: 201 us -> none  [the longest x3 36.2 us: body(): lax.all_to_all(rolled_parts[1], 'section', split_axis=0, concat_axis=0, t...]
    unnamed x55 -> x21, local copies, waits for them, and re-layouts: 169 us -> 0.7 us
    ppermute x1 -> x7, waiting for transfers between devices: 0.01 us -> 168 us  [the longest x4 168 us: mirror(): return lax.ppermute(block, 'section', mirror_route)]
    all_gather x1, waiting for transfers between devices: 0.01 us -> 60.4 us  [body(): gathered = lax.all_gather(swapped[:3 * tok], 'tensor', axis=1, tiled=True)]
    convert_element_type x3 -> x4, other arithmetic: 58.2 us -> 5.23 us  [the longest x2 3.36 us: block(): act = (preact * sigmoid).astype(BF16)]
    slice x6 -> x5, local copies, waits for them, and re-layouts: 50.5 us -> 2.4 us  [the longest x2 1.56 us: split_copies(): return jnp.concatenate([gathered[:, :half], gathered[:, half:]], 0)]
    all_to_all x8 -> x0, starting transfers between devices: 39.8 us -> none  [the longest x1 6.59 us: body(): lax.all_to_all(flattened[1], 'section', split_axis=0, concat_axis=0, tile...]
  transfers between devices with their start and end apart: 12 -> 10, of which waited for: 9 -> 7; matrix products, arithmetic and copies ran while one was open for 39% -> 5% of each run, Pallas kernels for 0% -> 0%
where the time goes in v1:
time: 348 us; the launch traced here: 343 us
  waiting for transfers between devices  272 us (78%)
  matrix products  24 us (7%)
  between operations  14 us (4%)
  blocking collectives  10.2 us (3%)
  starting transfers between devices  9.96 us (3%)
  other arithmetic  8.85 us (3%)
  local copies, waits for them, and re-layouts  4.09 us (1%)
    ppermute x4, waiting for transfers between devices, mirror(): return lax.ppermute(block, 'section', mirror_route)  168 us
    all_gather x1, waiting for transfers between devices, body(): gathered = lax.all_gather(swapped[:3 * tok], 'tensor', axis=1, tiled=True)  60.4 us
    reduce_scatter x2, waiting for transfers between devices, pass_down(): lax.psum_scatter(partial, 'tensor', scatter_dimension=1, tiled=True)  44 us
    dot_general x8, matrix products, dot(): lax.dot_general(left, right, (((left_dim,), (right_dim,)), ((), ())), pre...  24 us
    all_gather x1, blocking collectives, body(): grad1 = split_copies(lax.all_gather(incoming, 'tensor', axis=1, tiled=True))  10.2 us
    ppermute x4, starting transfers between devices, mirror(): return lax.ppermute(block, 'section', mirror_route)  7.18 us
  transfers between devices with their start and end apart: 10, of which 7 were waited for; matrix products, arithmetic and copies ran while one was open for 5% of the time, Pallas kernels for 0%

profile of v1, /device:TPU:0, one launch (start us, length us, event | category | flops | bytes accessed | tf_op | source)
XLA Modules:
  0.0 343.3 jit_solution(7874064468895706912)
XLA Ops:
  7.2 0.0 all-gather.2.cloned.1.call-start
  7.2 1.0 slice_bitcast_fusion.1
  8.2 1.0 select_bitcast_fusion
  9.2 0.9 pad_maximum_fusion
  10.1 0.7 collective-permute-start
  10.8 0.0 collective-permute-done
  10.9 0.8 slice.87
  11.6 0.0 all-gather.2.cloned.1.call-update
  11.7 0.0 reduce-scatter.3.cloned.1.call-start
  11.7 60.4 %all-gather.2.cloned.1.call-done = bf16[384,2048]{1,0:T(8,128)(2,1)} async-done(((bf16[384,512]{1,0:T(8,128)(2,1)}), bf16[384,2048]{1,0:T(8,128)(2,1)}) %all-gather.2.cloned.1.call-update) | async-done | bytes 1572880 | tf_op jit(solution)/shard_map/all_gather | solution.py:52
  72.1 1.5 fusion.68
  73.7 0.0 copy-start.3
  73.7 0.0 copy-start.4
  73.7 0.0 copy-start.2
  73.7 0.0 copy-start.1
  73.7 0.0 copy-start
  73.7 0.0 copy-start.8
  73.7 3.9 %fusion.12 = bf16[256,2048]{1,0:T(8,128)(2,1)S(1)} fusion(bf16[1,2048,1024]{2,1,0:T(8,128)(2,1)} %param.6, bf16[128,1024]{1,0:T(8,128)(2,1)S(1)} %get-tuple-element.11, bf16[128,1024]{1,0:T(8,128)(2,1)S(1)} %get-tuple-element.12), kind=kOutput, calls=%fused_computation.14 | convolution fusion | flops 1075314688 | bytes 5767168 | tf_op jit(solution)/shard_map/dot_general | solution.py:11
  77.7 0.0 copy-done.3
  77.7 0.0 copy-done.4
  77.7 2.5 collective-permute-start.1
  80.2 0.0 copy-done.2
  80.2 0.0 copy-done.8
  80.2 1.3 fusion.18
  81.4 0.0 copy-done.1
  81.5 0.6 collective-permute-start.2
  82.0 67.5 %collective-permute-done.1 = bf16[256,2048]{1,0:T(8,128)(2,1)S(1)} collective-permute-done((bf16[256,2048]{1,0:T(8,128)(2,1)S(1)}, bf16[256,2048]{1,0:T(8,128)(2,1)S(1)}, u32[]{:S(2)}, u32[]{:S(2)}) %collective-permute-start.1) | collective-permute-done | bytes 1048608 | tf_op jit(solution)/shard_map/ppermute | solution.py:43
  149.5 21.4 %collective-permute-done.2 = bf16[256,2048]{1,0:T(8,128)(2,1)S(1)} collective-permute-done((bf16[256,2048]{1,0:T(8,128)(2,1)S(1)}, bf16[256,2048]{1,0:T(8,128)(2,1)S(1)}, u32[]{:S(2)}, u32[]{:S(2)}) %collective-permute-start.2) | collective-permute-done | bytes 1048608 | tf_op jit(solution)/shard_map/ppermute | solution.py:43
  171.0 1.2 multiply_convert_fusion.1
  172.2 1.3 fusion.30
  173.5 0.8 pad_maximum_fusion.1
  174.4 0.0 reduce-scatter.3.cloned.1.call-update
  174.4 0.0 reduce-scatter.5.cloned.1.call-start
  174.4 24.9 %reduce-scatter.3.cloned.1.call-done = bf16[128,512]{1,0:T(8,128)(2,1)} async-done(((bf16[128,2048]{1,0:T(8,128)(2,1)}), bf16[128,512]{1,0:T(8,128)(2,1)}) %reduce-scatter.3.cloned.1.call-update) | async-done | bytes 131088 | tf_op jit(solution)/shard_map/reduce_scatter | solution.py:66
  199.3 0.9 add_convert_fusion.1
  200.3 1.3 collective-permute-start.3
  201.6 0.0 copy-done
  201.6 0.0 copy-start.7
  201.6 3.6 %fusion.21 = bf16[256,2048]{1,0:T(8,128)(2,1)S(1)} fusion(bf16[1,1024,2048]{2,1,0:T(8,128)(2,1)} %param.5, bf16[128,1024]{1,0:T(8,128)(2,1)S(1)} %get-tuple-element.8, bf16[128,1024]{1,0:T(8,128)(2,1)S(1)} %get-tuple-element.7), kind=kOutput, calls=%fused_computation.17 | convolution fusion | flops 1075314688 | bytes 5767168 | tf_op jit(solution)/shard_map/dot_general | solution.py:11
  205.2 3.1 collective-permute-start.5
  208.3 0.0 collective-permute-done.3
  208.3 10.2 %all_gather.7 = bf16[128,2048]{1,0:T(8,128)(2,1)S(1)} all-gather(bf16[128,512]{1,0:T(8,128)(2,1)S(1)} %slice_select_fusion), channel_id=1, replica_groups=mesh['section'=8,'tensor'=4] {'tensor'}, dimensions={1}, use_global_device_ids=true | all-gather | bytes 655360 | tf_op jit(solution)/shard_map/all_gather | solution.py:77
  218.6 0.0 copy-start.5
  218.6 0.0 copy-start.6
  218.6 0.0 copy-done.7
  218.6 1.3 fusion.15
  219.9 0.0 copy-done.5
  219.9 0.0 copy-done.6
  219.9 0.0 copy-start.9
  219.9 1.0 collective-permute-start.4
  221.0 56.2 %collective-permute-done.5 = bf16[256,2048]{1,0:T(8,128)(2,1)S(1)} collective-permute-done((bf16[256,2048]{1,0:T(8,128)(2,1)S(1)}, bf16[256,2048]{1,0:T(8,128)(2,1)S(1)}, u32[]{:S(2)}, u32[]{:S(2)}) %collective-permute-start.5) | collective-permute-done | bytes 1048608 | tf_op jit(solution)/shard_map/ppermute | solution.py:43
  277.2 22.5 %collective-permute-done.4 = bf16[256,2048]{1,0:T(8,128)(2,1)S(1)} collective-permute-done((bf16[256,2048]{1,0:T(8,128)(2,1)S(1)}, bf16[256,2048]{1,0:T(8,128)(2,1)S(1)}, u32[]{:S(2)}, u32[]{:S(2)}) %collective-permute-start.4) | collective-permute-done | bytes 1048608 | tf_op jit(solution)/shard_map/ppermute | solution.py:43
  299.7 2.1 multiply_convert_fusion
  301.8 0.0 copy-done.9
  301.8 1.3 fusion.33
  303.1 0.8 pad_maximum_fusion.2
  304.0 0.0 reduce-scatter.5.cloned.1.call-update
  304.0 5.9 %convert_bitcast_fusion = bf16[1,2048,1024]{2,1,0:T(8,128)(2,1)} fusion(bf16[256,2048]{1,0:T(8,128)(2,1)} %get-tuple-element.5, bf16[256,2048]{1,0:T(8,128)(2,1)S(1)} %get-tuple-element.3, bf16[128,1024]{1,0:T(8,128)(2,1)} %copy-done.6, bf16[128,1024]{1,0:T(8,128)(2,1)} %copy-done.5, bf16[128,1024]{1,0:T(8,128)(2,1)} %copy-done.3, ...), kind=kOutput, calls=%fused_computation.12 | convolution fusion | flops 2157969408 | bytes 7340032 | tf_op jit(solution)/shard_map/dot_general | solution.py:11
  309.9 19.1 %reduce-scatter.5.cloned.1.call-done = bf16[128,512]{1,0:T(8,128)(2,1)} async-done(((bf16[128,2048]{1,0:T(8,128)(2,1)}), bf16[128,512]{1,0:T(8,128)(2,1)}) %reduce-scatter.5.cloned.1.call-update) | async-done | bytes 131088 | tf_op jit(solution)/shard_map/reduce_scatter | solution.py:66
  329.0 0.9 add_convert_fusion
  330.0 0.7 collective-permute-start.6
  330.6 5.5 %convert_bitcast_fusion.1 = bf16[1,1024,2048]{2,1,0:T(8,128)(2,1)} fusion(bf16[256,2048]{1,0:T(8,128)(2,1)S(1)} %get-tuple-element.6, bf16[256,2048]{1,0:T(8,128)(2,1)S(1)} %get-tuple-element.4, bf16[128,1024]{1,0:T(8,128)(2,1)} %copy-done, bf16[128,1024]{1,0:T(8,128)(2,1)S(1)} %get-tuple-element.7, bf16[128,1024]{1,0:T(8,128)(2,1)} %copy-done.1, ...), kind=kOutput, calls=%fused_computation.13 | convolution fusion | flops 2157969408 | bytes 7340032 | tf_op jit(solution)/shard_map/dot_general | solution.py:11
  336.2 0.0 collective-permute-done.6
  336.2 0.7 copy.9
  (4 shorter events, 0.1 us)
Async XLA Ops:
  7.2 65.0 %all-gather.2.cloned.1.call-start = ((), (), s32[]{:S(2)}) async-start(), calls=%async_computation.2 | async-start | bytes 1966080 | tf_op jit(solution)/shard_map/all_gather | solution.py:52
  10.1 0.7 collective-permute-start
  11.7 187.7 %reduce-scatter.3.cloned.1.call-start = ((), (), s32[]{:S(2)}) async-start(), calls=%async_computation.3 | async-start | bytes 655360 | tf_op jit(solution)/shard_map/reduce_scatter | solution.py:66
  73.7 4.0 %copy-start.3 = (bf16[128,1024]{1,0:T(8,128)(2,1)}, bf16[128,1024]{1,0:T(8,128)(2,1)S(1)}, u32[]{:S(2)}) copy-start(bf16[128,1024]{1,0:T(8,128)(2,1)S(1)} %get-tuple-element.11) | copy-start | bytes 786436
  73.7 4.0 %copy-start.4 = (bf16[128,1024]{1,0:T(8,128)(2,1)}, bf16[128,1024]{1,0:T(8,128)(2,1)S(1)}, u32[]{:S(2)}) copy-start(bf16[128,1024]{1,0:T(8,128)(2,1)S(1)} %get-tuple-element.12) | copy-start | bytes 786436
  73.7 6.5 %copy-start.2 = (bf16[128,1024]{1,0:T(8,128)(2,1)}, bf16[128,1024]{1,0:T(8,128)(2,1)S(1)}, u32[]{:S(2)}) copy-start(bf16[128,1024]{1,0:T(8,128)(2,1)S(1)} %get-tuple-element.10) | copy-start | bytes 786436
  73.7 7.7 %copy-start.1 = (bf16[128,1024]{1,0:T(8,128)(2,1)}, bf16[128,1024]{1,0:T(8,128)(2,1)S(1)}, u32[]{:S(2)}) copy-start(bf16[128,1024]{1,0:T(8,128)(2,1)S(1)} %get-tuple-element.9) | copy-start | bytes 786436
  73.7 127.8 %copy-start = (bf16[128,1024]{1,0:T(8,128)(2,1)}, bf16[128,1024]{1,0:T(8,128)(2,1)S(1)}, u32[]{:S(2)}) copy-start(bf16[128,1024]{1,0:T(8,128)(2,1)S(1)} %get-tuple-element.8) | copy-start | bytes 786436
  73.7 6.5 %copy-start.8 = (bf16[1,1024,2048]{2,1,0:T(8,128)(2,1)S(1)}, bf16[1,1024,2048]{2,1,0:T(8,128)(2,1)}, u32[]{:S(2)}) copy-start(bf16[1,1024,2048]{2,1,0:T(8,128)(2,1)} %param.5) | copy-start | bytes 12582916
  77.7 71.8 %collective-permute-start.1 = (bf16[256,2048]{1,0:T(8,128)(2,1)S(1)}, bf16[256,2048]{1,0:T(8,128)(2,1)S(1)}, u32[]{:S(2)}, u32[]{:S(2)}) collective-permute-start(bf16[256,2048]{1,0:T(8,128)(2,1)S(1)} %fusion.12), channel_id=1, source_target_pairs={{0,16},{4,20},{8,24},{12,28},{16,0},{20,4},{24,8},{28,12},{1,17},{... | collective-permute-start | bytes 3145736 | tf_op jit(solution)/shard_map/ppermute | solution.py:43
  81.5 89.5 %collective-permute-start.2 = (bf16[256,2048]{1,0:T(8,128)(2,1)S(1)}, bf16[256,2048]{1,0:T(8,128)(2,1)S(1)}, u32[]{:S(2)}, u32[]{:S(2)}) collective-permute-start(bf16[256,2048]{1,0:T(8,128)(2,1)S(1)} %fusion.18), channel_id=1, source_target_pairs={{0,16},{4,20},{8,24},{12,28},{16,0},{20,4},{24,8},{28,12},{1,17},{... | collective-permute-start | bytes 3145736 | tf_op jit(solution)/shard_map/ppermute | solution.py:43
  174.4 154.6 %reduce-scatter.5.cloned.1.call-start = ((), (), s32[]{:S(2)}) async-start(), calls=%async_computation.4 | async-start | bytes 655360 | tf_op jit(solution)/shard_map/reduce_scatter | solution.py:66
  200.3 8.0 %collective-permute-start.3 = (bf16[128,512]{1,0:T(8,128)(2,1)S(1)}, bf16[128,512]{1,0:T(8,128)(2,1)S(1)}, u32[]{:S(2)}, u32[]{:S(2)}) collective-permute-start(bf16[128,512]{1,0:T(8,128)(2,1)S(1)} %add_convert_fusion.1), channel_id=1, source_target_pairs={{4,0},{8,4},{12,8},{16,12},{20,16},{24,20},{28,24},{5,1},{9,5},{13... | collective-permute-start | bytes 393224 | tf_op jit(solution)/shard_map/ppermute | solution.py:74
  201.6 17.0 %copy-start.7 = (bf16[1,2048,1024]{2,1,0:T(8,128)(2,1)S(1)}, bf16[1,2048,1024]{2,1,0:T(8,128)(2,1)}, u32[]{:S(2)}) copy-start(bf16[1,2048,1024]{2,1,0:T(8,128)(2,1)} %param.6) | copy-start | bytes 12582916
  205.2 72.0 %collective-permute-start.5 = (bf16[256,2048]{1,0:T(8,128)(2,1)S(1)}, bf16[256,2048]{1,0:T(8,128)(2,1)S(1)}, u32[]{:S(2)}, u32[]{:S(2)}) collective-permute-start(bf16[256,2048]{1,0:T(8,128)(2,1)S(1)} %fusion.21), channel_id=1, source_target_pairs={{0,16},{4,20},{8,24},{12,28},{16,0},{20,4},{24,8},{28,12},{1,17},{... | collective-permute-start | bytes 3145736 | tf_op jit(solution)/shard_map/ppermute | solution.py:43
  218.6 1.3 copy-start.5
  218.6 1.3 copy-start.6
  219.9 81.9 %copy-start.9 = (bf16[1,1024,2048]{2,1,0:T(8,128)(2,1)S(1)}, bf16[1,1024,2048]{2,1,0:T(8,128)(2,1)}, u32[]{:S(2)}) copy-start(bf16[1,1024,2048]{2,1,0:T(8,128)(2,1)} %param.5) | copy-start | bytes 12582916
  219.9 79.7 %collective-permute-start.4 = (bf16[256,2048]{1,0:T(8,128)(2,1)S(1)}, bf16[256,2048]{1,0:T(8,128)(2,1)S(1)}, u32[]{:S(2)}, u32[]{:S(2)}) collective-permute-start(bf16[256,2048]{1,0:T(8,128)(2,1)S(1)} %fusion.15), channel_id=1, source_target_pairs={{0,16},{4,20},{8,24},{12,28},{16,0},{20,4},{24,8},{28,12},{1,17},{... | collective-permute-start | bytes 3145736 | tf_op jit(solution)/shard_map/ppermute | solution.py:43
  330.0 6.2 %collective-permute-start.6 = (bf16[128,512]{1,0:T(8,128)(2,1)S(1)}, bf16[128,512]{1,0:T(8,128)(2,1)S(1)}, u32[]{:S(2)}, u32[]{:S(2)}) collective-permute-start(bf16[128,512]{1,0:T(8,128)(2,1)S(1)} %add_convert_fusion), channel_id=1, source_target_pairs={{0,0},{1,1},{2,16},{3,17},{4,4},{5,5},{6,20},{7,21},{8,8},{9,9},{1... | collective-permute-start | bytes 393224 | tf_op jit(solution)/shard_map/ppermute | solution.py:40
Sparse Core Ops, SparseCore 0:
  11.8 60.3 all-gather.1
  174.5 24.7 reduce-scatter.2
  304.1 24.8 reduce-scatter.4

commit v2 on v1

v2 whole, which is shorter than its diff:
```python
import functools

import jax
import jax.numpy as jnp
from jax import lax
from jax.experimental import pallas as pl
from jax.experimental.pallas import tpu as pltpu
from jax.sharding import PartitionSpec as P

F32 = jnp.float32
BF16 = jnp.bfloat16
MESH = pl.DeviceIdType.MESH
X0, X1, G0, G1 = 0, 1, 2, 3
P0, Q0, P1, Q1 = 0, 1, 2, 3


def dot(left, right, left_dim, right_dim):
    return lax.dot_general(
        left, right, (((left_dim,), (right_dim,)), ((), ())), preferred_element_type=F32
    )


def tiled(width, tile, step):
    tile = min(tile, width)

    @pl.loop(0, width // tile)
    def _(j):
        step(pl.ds(pl.multiple_of(j * tile, tile), tile))


def chain(
    sections, tensors,
    value_hbm, out_hbm, saved, first, head,
    xg_out, act_out, pre_out, passed_out,
    wv, wo, inb, ob, rb, act, pre, part, rs, rel,
    w_sem, loc_sem, fin_sem,
    own_s, own_r, swp_s, swp_r, oth_s, oth_r, x_s, x_r, rs_s, rs_r, g1_s, g1_r, hd_s, hd_r,
):
    copies, low = sections // 2, tensors // 2
    position, t = lax.axis_index("section"), lax.axis_index("tensor")
    side, s = position // copies, lax.rem(position, copies)
    h, i = t // low, lax.rem(t, low)
    tok, chunk = first.shape
    inner = wv.shape[1]
    rows = tok // 2
    home = h == side
    away = jnp.logical_not(home)
    at_end = s == copies - 1
    mirror = (lax.rem(position + copies, sections), t)
    swap_to = (h * copies + s, side * low + i)
    mine_rel = jnp.where(home, 0, 1)

    def peer(d):
        return (position, lax.rem(t + d, tensors))

    def cols(k):
        return pl.ds(pl.multiple_of(k * chunk, chunk), chunk)

    def remote(src, dst, send, recv, device):
        return pltpu.make_async_remote_copy(
            src_ref=src, dst_ref=dst, send_sem=send, recv_sem=recv,
            device_id=device, device_id_type=MESH,
        )

    def arrived(dst, recv):
        remote(dst, dst, own_s.at[0, 0], recv, mirror).wait_recv()

    pending = []

    def send(copy, when=None):
        if when is None:
            copy().start()
        else:
            @pl.when(when)
            def _():
                copy().start()
        pending.append((copy, when))

    load_v = pltpu.make_async_copy(value_hbm, wv, w_sem.at[0])
    load_o = pltpu.make_async_copy(out_hbm, wo, w_sem.at[1])
    load_v.start()
    load_o.start()

    barrier = pltpu.get_barrier_semaphore()

    def greet(device):
        pl.semaphore_signal(barrier, inc=1, device_id=device, device_id_type=MESH)

    greet(mirror)
    for d in range(1, tensors):
        greet(peer(d))

    @pl.when(away)
    def _():
        greet(swap_to)

    @pl.when(s > 0)
    def _():
        for u in range(tensors):
            greet((position - 1, u))

    @pl.when(s < copies - 1)
    def _():
        for u in range(tensors):
            greet((position + 1, u))

    greeted = tensors + jnp.where(away, 1, 0)
    greeted += jnp.where(s > 0, tensors, 0) + jnp.where(s < copies - 1, tensors, 0)
    pl.semaphore_wait(barrier, greeted)

    source = {X0: saved.at[0], X1: saved.at[1], G0: first}
    order = (X0, G0, X1)

    for k in order:
        for way, target in ((0, mirror), (1, swap_to)):
            part_rows = pl.ds(way * rows, rows)
            send(lambda k=k, way=way, target=target, part_rows=part_rows: remote(
                source[k].at[part_rows, :], inb.at[k, 1, part_rows, cols(i)],
                swp_s.at[k, way], swp_r.at[k], target), away)
    for k in order:
        for d in range(1, tensors):
            send(lambda k=k, d=d: remote(
                source[k], inb.at[k, 0, :, cols(i)],
                own_s.at[k, d - 1], own_r.at[k, i], peer(d)), home)

        @pl.when(home)
        def _(k=k):
            pltpu.make_async_copy(source[k], inb.at[k, 0, :, cols(i)], loc_sem.at[k]).start()

    def head_copy(d, rel_slot):
        which = side if rel_slot == 0 else 1 - side
        return remote(
            head.at[which], inb.at[G1, rel_slot, :, cols(i)],
            hd_s.at[rel_slot, d - 1], hd_r.at[rel_slot, i], peer(d))

    head_home = jnp.logical_and(home, at_end)

    def own_block(k):
        for j in range(low):
            u = side * low + j

            @pl.when(u == t)
            def _():
                pltpu.make_async_copy(source[k], inb.at[k, 0, :, cols(j)], loc_sem.at[k]).wait()

            @pl.when(u != t)
            def _():
                arrived(inb.at[k, 0, :, cols(j)], own_r.at[k, j])

    def project(kind, k, slot):
        def step(c):
            if kind in (P0, P1):
                value = dot(inb[k, slot], wv[:, c], 1, 0)
            else:
                value = dot(inb[k, slot], wo[c, :], 1, 1)
            ob[kind, slot, :, c] = value.astype(BF16)

        tiled(inner, 512, step)

    def exchange(kind, slot):
        send(lambda: remote(
            ob.at[kind, slot], rb.at[kind, 1 - slot],
            x_s.at[kind, slot], x_r.at[kind, 1 - slot], mirror))

    own_block(X0)
    load_v.wait()
    project(P0, X0, 0)
    exchange(P0, 0)
    own_block(G0)
    load_o.wait()
    project(Q0, G0, 0)
    exchange(Q0, 0)

    row_mine = pl.ds(pl.multiple_of(mine_rel * rows, rows), rows)
    for k in order:
        arrived(inb.at[k, 1, row_mine, cols(i)], swp_r.at[k])
        for d in range(1, tensors):
            send(lambda k=k, d=d: remote(
                inb.at[k, 1, row_mine, cols(i)], inb.at[k, 1, row_mine, cols(i)],
                oth_s.at[k, d - 1], oth_r.at[k, d - 1], peer(d)))

    def other_block(k):
        for d in range(1, tensors):
            u = lax.rem(t + tensors - d, tensors)
            r = pl.multiple_of(jnp.where(u // low == side, 0, rows), rows)
            arrived(inb.at[k, 1, pl.ds(r, rows), cols(lax.rem(u, low))], oth_r.at[k, d - 1])

    other_block(X0)
    project(P0, X0, 1)
    exchange(P0, 1)
    other_block(G0)
    project(Q0, G0, 1)
    exchange(Q0, 1)
    own_block(X1)
    project(P1, X1, 0)
    other_block(X1)
    project(P1, X1, 1)

    for rel_slot in range(2):
        for d in range(1, tensors):
            send(functools.partial(head_copy, d, rel_slot), head_home)

        @pl.when(head_home)
        def _(rel_slot=rel_slot):
            which = side if rel_slot == 0 else 1 - side
            pltpu.make_async_copy(
                head.at[which], inb.at[G1, rel_slot, :, cols(i)], loc_sem.at[3 + rel_slot]).start()

    def unit(tick, slot):
        p_kind, q_kind = (P0, Q0) if tick == 0 else (P1, Q1)
        arrived(rb.at[p_kind, slot], x_r.at[p_kind, slot])
        arrived(rb.at[q_kind, slot], x_r.at[q_kind, slot])

        def bend(c):
            p = ob[p_kind, slot, :, c].astype(F32) + rb[p_kind, slot, :, c].astype(F32)
            q = ob[q_kind, slot, :, c].astype(F32) + rb[q_kind, slot, :, c].astype(F32)
            sigmoid = jax.nn.sigmoid(p)
            act[tick, slot, :, c] = (p * sigmoid).astype(BF16)
            pre[tick, slot, :, c] = (q * (sigmoid * (1.0 + p * (1.0 - sigmoid)))).astype(BF16)

        tiled(inner, 256, bend)

        def back(c):
            part[tick, slot, :, c] = dot(pre[tick, slot], wv[c, :], 1, 1).astype(BF16)

        tiled(wv.shape[0], 256, back)
        for j in range(low):
            u = (side if slot == 0 else 1 - side) * low + j
            d = lax.rem(t - u + tensors, tensors)
            lane = jnp.maximum(d - 1, 0)
            send(lambda u=u, lane=lane, j=j: remote(
                part.at[tick, slot, :, cols(j)], rs.at[tick, lane],
                rs_s.at[tick, slot, j], rs_r.at[tick, lane], (position, u)), d != 0)

    def reduce(tick, incoming):
        total = part[tick, mine_rel, :, cols(i)].astype(F32)
        for d in range(1, tensors):
            arrived(rs.at[tick, d - 1], rs_r.at[tick, d - 1])
            total += rs[tick, d - 1].astype(F32)
        rel[tick] = (inb[incoming, mine_rel, :, cols(i)].astype(F32) + total).astype(BF16)

    unit(0, 1)
    exchange(P1, 0)
    unit(0, 0)
    exchange(P1, 1)
    reduce(0, G0)
    for u in range(tensors):
        send(lambda u=u: remote(
            rel.at[0], inb.at[G1, mine_rel, :, cols(i)],
            g1_s.at[u], g1_r.at[t], (position - 1, u)), s > 0)

    @pl.when(at_end)
    def _():
        for rel_slot in range(2):
            for j in range(low):
                u = side * low + j

                @pl.when(u == t)
                def _():
                    which = side if rel_slot == 0 else 1 - side
                    pltpu.make_async_copy(
                        head.at[which], inb.at[G1, rel_slot, :, cols(j)],
                        loc_sem.at[3 + rel_slot]).wait()

                @pl.when(u != t)
                def _():
                    arrived(inb.at[G1, rel_slot, :, cols(j)], hd_r.at[rel_slot, j])

    @pl.when(jnp.logical_not(at_end))
    def _():
        for u in range(tensors):
            r = jnp.where(u // low == side, 0, 1)
            arrived(inb.at[G1, r, :, cols(u % low)], g1_r.at[u])

    for slot in range(2):
        project(Q1, G1, slot)
        exchange(Q1, slot)
    xg_copy = pltpu.make_async_copy(inb, xg_out, fin_sem.at[0])
    xg_copy.start()
    unit(1, 1)
    unit(1, 0)
    act_copy = pltpu.make_async_copy(act, act_out, fin_sem.at[1])
    pre_copy = pltpu.make_async_copy(pre, pre_out, fin_sem.at[2])
    act_copy.start()
    pre_copy.start()
    reduce(1, G1)
    passed_copy = pltpu.make_async_copy(rel.at[1], passed_out, fin_sem.at[3])
    passed_copy.start()
    for copy, when in pending:
        if when is None:
            copy().wait_send()
        else:
            @pl.when(when)
            def _():
                copy().wait_send()
    for copy in (xg_copy, act_copy, pre_copy, passed_copy):
        copy.wait()


def body(value_half, out_half, saved, first_grad, head_grad):
    sections, tensors = lax.axis_size("section"), lax.axis_size("tensor")
    copies, low = sections // 2, tensors // 2
    half, inner = value_half.shape[1:]
    tok, chunk = first_grad.shape[1:]
    dma = pltpu.SemaphoreType.DMA
    hbm, vmem = pl.BlockSpec(memory_space=pl.ANY), pl.BlockSpec(memory_space=pltpu.VMEM)
    shape = jax.ShapeDtypeStruct
    xg, act, pre, passed = pl.pallas_call(
        functools.partial(chain, sections, tensors),
        out_shape=(
            shape((4, 2, tok, half), BF16),
            shape((2, 2, tok, inner), BF16),
            shape((2, 2, tok, inner), BF16),
            shape((tok, chunk), BF16),
        ),
        in_specs=[hbm, hbm, vmem, vmem, vmem],
        out_specs=(hbm, hbm, hbm, hbm),
        scratch_shapes=[
            pltpu.VMEM((half, inner), BF16),
            pltpu.VMEM((inner, half), BF16),
            pltpu.VMEM((4, 2, tok, half), BF16),
            pltpu.VMEM((4, 2, tok, inner), BF16),
            pltpu.VMEM((4, 2, tok, inner), BF16),
            pltpu.VMEM((2, 2, tok, inner), BF16),
            pltpu.VMEM((2, 2, tok, inner), BF16),
            pltpu.VMEM((2, 2, tok, half), BF16),
            pltpu.VMEM((2, tensors - 1, tok, chunk), BF16),
            pltpu.VMEM((2, tok, chunk), BF16),
            dma((2,)), dma((5,)), dma((4,)),
            dma((3, tensors - 1)), dma((3, low)),
            dma((3, 2)), dma((3,)),
            dma((3, tensors - 1)), dma((3, tensors - 1)),
            dma((4, 2)), dma((4, 2)),
            dma((2, 2, low)), dma((2, tensors - 1)),
            dma((tensors,)), dma((tensors,)),
            dma((2, tensors - 1)), dma((2, low)),
        ],
        compiler_params=pltpu.CompilerParams(
            collective_id=0, has_side_effects=True, vmem_limit_bytes=48 * 2**20
        ),
        cost_estimate=pl.CostEstimate(
            flops=24 * tok * half * inner, bytes_accessed=8 * half * inner, transcendentals=4 * tok * inner
        ),
    )(value_half[0], out_half[0], saved[0], first_grad[0], head_grad)

    swap_route = []
    for r in range(sections):
        for t in range(tensors):
            c, s, h, i = r // copies, r % copies, t // low, t % low
            swap_route.append((r * tensors + t, (h * copies + s) * tensors + c * low + i))
    sent = lax.ppermute(passed, ("section", "tensor"), swap_route)
    inputs = xg[:2].reshape(4 * tok, half)
    grads = xg[2:].reshape(4 * tok, half)
    value_grad = dot(inputs, pre.reshape(4 * tok, inner), 0, 0).astype(BF16)
    out_grad = dot(act.reshape(4 * tok, inner), grads, 0, 0).astype(BF16)
    return sent[None], value_grad[None], out_grad[None]


def solution(mesh):
    return jax.shard_map(
        body,
        mesh=mesh,
        in_specs=(
            P("section", None, "tensor"),
            P("section", "tensor", None),
            P("section", None, None, "tensor"),
            P("section", None, "tensor"),
            P(None, None, "tensor"),
        ),
        out_specs=(
            P("section", None, "tensor"),
            P("section", None, "tensor"),
            P("section", "tensor", None),
        ),
        check_vma=False,
    )
```

time: 348 us -> 228 us (0.66); the launches traced: 343 us -> 228 us
  waiting for transfers between devices: 272 us -> 0.01 us
  Pallas kernels: 0 us -> 213 us
  matrix products: 24 us -> 10.4 us
  between operations: 14 us -> 0.66 us
  blocking collectives: 10.2 us -> 0 us
  starting transfers between devices: 9.96 us -> 0.67 us
  other arithmetic: 8.85 us -> 0 us
    pallas_call x0 -> x1, Pallas kernels: none -> 213 us  [body(): pl.pallas_call(functools.partial(chain, sections, tensors), out_shape=(sh...]
    ppermute x7 -> x1, waiting for transfers between devices: 168 us -> 0.01 us  [body(): sent = lax.ppermute(passed, ('section', 'tensor'), swap_route)]
    all_gather x1 -> x0, waiting for transfers between devices: 60.4 us -> none  [body(): gathered = lax.all_gather(swapped[:3 * tok], 'tensor', axis=1, tiled=True)]
    reduce_scatter x2 -> x0, waiting for transfers between devices: 44 us -> none  [pass_down(): lax.psum_scatter(partial, 'tensor', scatter_dimension=1, tiled=True)]
    dot_general x8 -> x2, matrix products: 24 us -> 10.4 us  [dot(): lax.dot_general(left, right, (((left_dim,), (right_dim,)), ((), ())), pre...]
    all_gather x1 -> x0, blocking collectives: 10.2 us -> none  [body(): grad1 = split_copies(lax.all_gather(incoming, 'tensor', axis=1, tiled=True))]
    ppermute x7 -> x1, starting transfers between devices: 9.83 us -> 0.67 us  [body(): sent = lax.ppermute(passed, ('section', 'tensor'), swap_route)]
    convert_element_type x4 -> x0, other arithmetic: 5.23 us -> none  [the longest x2 3.36 us: block(): act = (preact * sigmoid).astype(BF16)]
  transfers between devices with their start and end apart: 10 -> 1, of which waited for: 7 -> 0; matrix products, arithmetic and copies ran while one was open for 5% -> 5% of each run, Pallas kernels for 0% -> 0%
where the time goes in v2:
time: 228 us
  Pallas kernels  213 us (93%)
  matrix products  10.4 us (5%)
  local copies, waits for them, and re-layouts  3.45 us (2%)
    pallas_call x1, Pallas kernels, body(): pl.pallas_call(functools.partial(chain, sections, tensors), out_shape=(sh...  213 us
    dot_general x2, matrix products, dot(): lax.dot_general(left, right, (((left_dim,), (right_dim,)), ((), ())), pre...  10.4 us
  transfers between devices with their start and end apart: 1, of which 0 were waited for; matrix products, arithmetic and copies ran while one was open for 5% of the time, Pallas kernels for 0%

profile of v2, /device:TPU:0, one launch (start us, length us, event | category | flops | bytes accessed | tf_op | source)
XLA Modules:
  0.0 227.7 jit_solution(13424307324439565751)
XLA Ops:
  0.6 0.0 copy-start
  0.6 0.9 copy-done
  1.6 0.0 copy-start.1
  1.6 0.9 copy-done.1
  2.5 0.0 copy-start.2
  2.5 0.9 copy-done.2
  3.4 212.5 %shard_map.76 = (bf16[4,2,128,1024]{3,2,1,0:T(8,128)(2,1)S(1)}, bf16[2,2,128,2048]{3,2,1,0:T(8,128)(2,1)S(1)}, bf16[2,2,128,2048]{3,2,1,0:T(8,128)(2,1)}, bf16[128,512]{1,0:T(8,128)(2,1)S(1)}) custom-call(bf16[1024,2048]{1,0:T(8,128)(2,1)} %bitcast.27, bf16[2048,1024]{1,0:T(8,128)(2,1)} %bitcast.28, bf16[2,128,512]{2,1,0:T(8,128)(2,1)S(1)} %bitcast.24, ...), custom_call_target="tpu_custom_call" | custom-call | flops 6442450944 | bytes 16777216 | tf_op jit(solution)/shard_map/pallas_call | solution.py:308
  216.0 0.7 collective-permute-start
  216.7 6.0 %fusion = bf16[1,1024,2048]{2,1,0:T(8,128)(2,1)} fusion(bf16[4,2,128,1024]{3,2,1,0:T(8,128)(2,1)S(1)} %get-tuple-element.8, bf16[2,2,128,2048]{3,2,1,0:T(8,128)(2,1)} %get-tuple-element.9), kind=kOutput, calls=%fused_computation.2 | convolution fusion | flops 2149580800 | bytes 8388608 | tf_op jit(solution)/shard_map/dot_general | solution.py:18
  222.7 4.4 %fusion.1 = bf16[1,2048,1024]{2,1,0:T(8,128)(2,1)} fusion(bf16[2,2,128,2048]{3,2,1,0:T(8,128)(2,1)S(1)} %get-tuple-element.10, bf16[4,2,128,1024]{3,2,1,0:T(8,128)(2,1)S(1)} %get-tuple-element.8), kind=kOutput, calls=%fused_computation.3 | convolution fusion | flops 2149580800 | bytes 7340032 | tf_op jit(solution)/shard_map/dot_general | solution.py:18
  227.0 0.0 collective-permute-done
  227.0 0.7 copy.15
Async XLA Ops:
  0.6 1.0 copy-start
  1.6 0.9 copy-start.1
  2.5 0.9 copy-start.2
  216.0 11.1 %collective-permute-start = (bf16[128,512]{1,0:T(8,128)(2,1)S(1)}, bf16[128,512]{1,0:T(8,128)(2,1)S(1)}, u32[]{:S(2)}, u32[]{:S(2)}) collective-permute-start(bf16[128,512]{1,0:T(8,128)(2,1)S(1)} %get-tuple-element.7), channel_id=1, source_target_pairs={{0,0},{1,1},{2,16},{3,17},{4,4},{5,5},{6,20},{7,21},{8,8},{9,9},{1... | collective-permute-start | bytes 393224 | tf_op jit(solution)/shard_map/ppermute | solution.py:351

commit v3 on v2

--- a/solution.py
+++ b/solution.py
@@ -31,8 +31,8 @@
 def chain(
     sections, tensors,
     value_hbm, out_hbm, saved, first, head,
-    xg_out, act_out, pre_out, passed_out,
-    wv, wo, inb, ob, rb, act, pre, part, rs, rel,
+    xg_out, act_out, pre_out, value_out, wide_out, passed_out,
+    wv, wo, vg, og, inb, ob, rb, act, pre, part, rs, rel,
     w_sem, loc_sem, fin_sem,
     own_s, own_r, swp_s, swp_r, oth_s, oth_r, x_s, x_r, rs_s, rs_r, g1_s, g1_r, hd_s, hd_r,
 ):
@@ -157,10 +157,13 @@
 
         tiled(inner, 512, step)
 
+    def product(kind, slot):
+        return remote(
+            ob.at[kind, slot], rb.at[kind, 1 - slot],
+            x_s.at[kind, slot], x_r.at[kind, 1 - slot], mirror)
+
     def exchange(kind, slot):
-        send(lambda: remote(
-            ob.at[kind, slot], rb.at[kind, 1 - slot],
-            x_s.at[kind, slot], x_r.at[kind, 1 - slot], mirror))
+        send(functools.partial(product, kind, slot))
 
     own_block(X0)
     load_v.wait()
@@ -193,6 +196,7 @@
     exchange(Q0, 1)
     own_block(X1)
     project(P1, X1, 0)
+    exchange(P1, 0)
     other_block(X1)
     project(P1, X1, 1)
 
@@ -206,10 +210,11 @@
             pltpu.make_async_copy(
                 head.at[which], inb.at[G1, rel_slot, :, cols(i)], loc_sem.at[3 + rel_slot]).start()
 
-    def unit(tick, slot):
+    def unit(tick, slot, on_arrival=lambda: None):
         p_kind, q_kind = (P0, Q0) if tick == 0 else (P1, Q1)
         arrived(rb.at[p_kind, slot], x_r.at[p_kind, slot])
         arrived(rb.at[q_kind, slot], x_r.at[q_kind, slot])
+        on_arrival()
 
         def bend(c):
             p = ob[p_kind, slot, :, c].astype(F32) + rb[p_kind, slot, :, c].astype(F32)
@@ -239,10 +244,8 @@
             total += rs[tick, d - 1].astype(F32)
         rel[tick] = (inb[incoming, mine_rel, :, cols(i)].astype(F32) + total).astype(BF16)
 
-    unit(0, 1)
-    exchange(P1, 0)
+    unit(0, 1, lambda: exchange(P1, 1))
     unit(0, 0)
-    exchange(P1, 1)
     reduce(0, G0)
     for u in range(tensors):
         send(lambda u=u: remote(
@@ -272,20 +275,40 @@
             r = jnp.where(u // low == side, 0, 1)
             arrived(inb.at[G1, r, :, cols(u % low)], g1_r.at[u])
 
-    for slot in range(2):
-        project(Q1, G1, slot)
-        exchange(Q1, slot)
-    xg_copy = pltpu.make_async_copy(inb, xg_out, fin_sem.at[0])
-    xg_copy.start()
-    unit(1, 1)
-    unit(1, 0)
-    act_copy = pltpu.make_async_copy(act, act_out, fin_sem.at[1])
-    pre_copy = pltpu.make_async_copy(pre, pre_out, fin_sem.at[2])
-    act_copy.start()
-    pre_copy.start()
+    local = []
+
+    def store(src, dst):
+        copy = pltpu.make_async_copy(src, dst, fin_sem.at[len(local)])
+        copy.start()
+        local.append(copy)
+
+    def flat(ref):
+        return ref.reshape(2 * tok, ref.shape[-1])
+
+    project(Q1, G1, 0)
+    product(Q1, 0).start()
+    project(Q1, G1, 1)
+    store(inb.at[X1], xg_out.at[0])
+    store(inb.at[G1], xg_out.at[1])
+
+    def value_term(c):
+        vg[:, c] = dot(flat(inb[X0]), flat(pre[0, :, :, c]), 0, 0).astype(BF16)
+
+    def wide_term(c):
+        og[c, :] = dot(flat(act[0, :, :, c]), flat(inb[G0]), 0, 0).astype(BF16)
+
+    tiled(inner, 256, value_term)
+    store(vg, value_out)
+    tiled(inner, 256, wide_term)
+    store(og, wide_out)
+    product(Q1, 0).wait_send()
+    exchange(Q1, 1)
+    for slot in (1, 0):
+        unit(1, slot)
+        store(act.at[1, slot], act_out.at[slot])
+        store(pre.at[1, slot], pre_out.at[slot])
     reduce(1, G1)
-    passed_copy = pltpu.make_async_copy(rel.at[1], passed_out, fin_sem.at[3])
-    passed_copy.start()
+    store(rel.at[1], passed_out)
     for copy, when in pending:
         if when is None:
             copy().wait_send()
@@ -293,7 +316,7 @@
             @pl.when(when)
             def _():
                 copy().wait_send()
-    for copy in (xg_copy, act_copy, pre_copy, passed_copy):
+    for copy in local:
         copy.wait()
 
 
@@ -303,19 +326,23 @@
     half, inner = value_half.shape[1:]
     tok, chunk = first_grad.shape[1:]
     dma = pltpu.SemaphoreType.DMA
-    hbm, vmem = pl.BlockSpec(memory_space=pl.ANY), pl.BlockSpec(memory_space=pltpu.VMEM)
+    hbm = pl.BlockSpec(memory_space=pl.ANY)
     shape = jax.ShapeDtypeStruct
-    xg, act, pre, passed = pl.pallas_call(
+    xg, act, pre, value0, wide0, passed = pl.pallas_call(
         functools.partial(chain, sections, tensors),
         out_shape=(
-            shape((4, 2, tok, half), BF16),
-            shape((2, 2, tok, inner), BF16),
-            shape((2, 2, tok, inner), BF16),
+            shape((2, 2, tok, half), BF16),
+            shape((2, tok, inner), BF16),
+            shape((2, tok, inner), BF16),
+            shape((half, inner), BF16),
+            shape((inner, half), BF16),
             shape((tok, chunk), BF16),
         ),
-        in_specs=[hbm, hbm, vmem, vmem, vmem],
-        out_specs=(hbm, hbm, hbm, hbm),
+        in_specs=[hbm] * 5,
+        out_specs=(hbm,) * 6,
         scratch_shapes=[
+            pltpu.VMEM((half, inner), BF16),
+            pltpu.VMEM((inner, half), BF16),
             pltpu.VMEM((half, inner), BF16),
             pltpu.VMEM((inner, half), BF16),
             pltpu.VMEM((4, 2, tok, half), BF16),
@@ -326,7 +353,7 @@
             pltpu.VMEM((2, 2, tok, half), BF16),
             pltpu.VMEM((2, tensors - 1, tok, chunk), BF16),
             pltpu.VMEM((2, tok, chunk), BF16),
-            dma((2,)), dma((5,)), dma((4,)),
+            dma((2,)), dma((5,)), dma((9,)),
             dma((3, tensors - 1)), dma((3, low)),
             dma((3, 2)), dma((3,)),
             dma((3, tensors - 1)), dma((3, tensors - 1)),
@@ -349,10 +376,11 @@
             c, s, h, i = r // copies, r % copies, t // low, t % low
             swap_route.append((r * tensors + t, (h * copies + s) * tensors + c * low + i))
     sent = lax.ppermute(passed, ("section", "tensor"), swap_route)
-    inputs = xg[:2].reshape(4 * tok, half)
-    grads = xg[2:].reshape(4 * tok, half)
-    value_grad = dot(inputs, pre.reshape(4 * tok, inner), 0, 0).astype(BF16)
-    out_grad = dot(act.reshape(4 * tok, inner), grads, 0, 0).astype(BF16)
+    inputs, grads = xg[0].reshape(2 * tok, half), xg[1].reshape(2 * tok, half)
+    value1 = dot(inputs, pre.reshape(2 * tok, inner), 0, 0)
+    wide1 = dot(act.reshape(2 * tok, inner), grads, 0, 0)
+    value_grad = (value0.astype(F32) + value1).astype(BF16)
+    out_grad = (wide0.astype(F32) + wide1).astype(BF16)
     return sent[None], value_grad[None], out_grad[None]
 
 

time: 228 us -> 227 us (level)
  transfers between devices with their start and end apart: 1 -> 1, of which waited for: 0 -> 0; matrix products, arithmetic and copies ran while one was open for 5% -> 4% of each run, Pallas kernels for 0% -> 0%
where the time goes in v3:
time: 227 us
  Pallas kernels  213 us (94%)
  matrix products  8.95 us (4%)
  local copies, waits for them, and re-layouts  3.53 us (2%)
    pallas_call x1, Pallas kernels, body(): pl.pallas_call(functools.partial(chain, sections, tensors), out_shape=(sh...  213 us
    dot_general x2, matrix products, dot(): lax.dot_general(left, right, (((left_dim,), (right_dim,)), ((), ())), pre...  8.95 us
  transfers between devices with their start and end apart: 1, of which 0 were waited for; matrix products, arithmetic and copies ran while one was open for 4% of the time, Pallas kernels for 0%

profile of v3, /device:TPU:0, one launch (start us, length us, event | category | flops | bytes accessed | tf_op | source)
XLA Modules:
  0.0 227.1 jit_solution(12241065909974246067)
XLA Ops:
  0.6 0.0 copy-start
  0.6 0.9 copy-done
  1.6 0.0 copy-start.1
  1.6 0.9 copy-done.1
  2.5 0.0 copy-start.2
  2.5 0.9 copy-done.2
  3.4 213.2 %shard_map.76 = (bf16[2,2,128,1024]{3,2,1,0:T(8,128)(2,1)S(1)}, bf16[2,128,2048]{2,1,0:T(8,128)(2,1)S(1)}, bf16[2,128,2048]{2,1,0:T(8,128)(2,1)S(1)}, bf16[1024,...) custom-call(bf16[1024,2048]{1,0:T(8,128)(2,1)} %bitcast.24, ...), custom_call_target="tpu_custom_call" | custom-call | flops 6442450944 | bytes 16777216 | tf_op jit(solution)/shard_map/pallas_call | solution.py:331
  216.7 0.7 collective-permute-start
  217.3 0.1 fusion.2
  217.4 0.0 copy-start.3
  217.4 5.6 %fusion.1 = bf16[1,2048,1024]{2,1,0:T(8,128)(2,1)} fusion(bf16[256,2048]{1,0:T(8,128)(2,1)S(1)} %bitcast.20, bf16[256,1024]{1,0:T(8,128)(2,1)S(1)} %bitcast.22, bf16[2048,1024]{1,0:T(8,128)(2,1)} %get-tuple-element.13), kind=kOutput, calls=%fused_computation.3 | convolution fusion | flops 1080033280 | bytes 9961472 | tf_op jit(solution)/shard_map/dot_general | solution.py:18
  223.1 0.0 copy-done.3
  223.1 3.3 %fusion = bf16[1,1024,2048]{2,1,0:T(8,128)(2,1)} fusion(bf16[256,1024]{1,0:T(8,128)(2,1)S(1)} %bitcast.21, bf16[256,2048]{1,0:T(8,128)(2,1)S(1)} %bitcast.19, bf16[1024,2048]{1,0:T(8,128)(2,1)S(1)} %copy-done.3), kind=kOutput, calls=%fused_computation.2 | convolution fusion | flops 1080033280 | bytes 9961472 | tf_op jit(solution)/shard_map/dot_general | solution.py:18
  226.4 0.0 collective-permute-done
  226.4 0.7 copy.9
Async XLA Ops:
  0.6 1.0 copy-start
  1.6 0.9 copy-start.1
  2.5 0.9 copy-start.2
  216.7 9.7 %collective-permute-start = (bf16[128,512]{1,0:T(8,128)(2,1)S(1)}, bf16[128,512]{1,0:T(8,128)(2,1)S(1)}, u32[]{:S(2)}, u32[]{:S(2)}) collective-permute-start(bf16[128,512]{1,0:T(8,128)(2,1)S(1)} %get-tuple-element.9), channel_id=1, source_target_pairs={{0,0},{1,1},{2,16},{3,17},{4,4},{5,5},{6,20},{7,21},{8,8},{9,9},{1... | collective-permute-start | bytes 393224 | tf_op jit(solution)/shard_map/ppermute | solution.py:378
  217.4 5.7 %copy-start.3 = (bf16[1024,2048]{1,0:T(8,128)(2,1)S(1)}, bf16[1024,2048]{1,0:T(8,128)(2,1)}, u32[]{:S(2)}) copy-start(bf16[1024,2048]{1,0:T(8,128)(2,1)} %get-tuple-element.10) | copy-start | bytes 12582916

commit v4 on v3

--- a/solution.py
+++ b/solution.py
@@ -32,9 +32,9 @@
     sections, tensors,
     value_hbm, out_hbm, saved, first, head,
     xg_out, act_out, pre_out, value_out, wide_out, passed_out,
-    wv, wo, vg, og, inb, ob, rb, act, pre, part, rs, rel,
+    wv, wo, vg, og, inb, via, ob, rb, act, pre, part, rs, rel,
     w_sem, loc_sem, fin_sem,
-    own_s, own_r, swp_s, swp_r, oth_s, oth_r, x_s, x_r, rs_s, rs_r, g1_s, g1_r, hd_s, hd_r,
+    own_s, own_r, swp_s, swp_r, via_s, via_r, oth_s, oth_r, x_s, x_r, rs_s, rs_r, g1_s, g1_r, hd_s, hd_r,
 ):
     copies, low = sections // 2, tensors // 2
     position, t = lax.axis_index("section"), lax.axis_index("tensor")
@@ -47,7 +47,7 @@
     away = jnp.logical_not(home)
     at_end = s == copies - 1
     mirror = (lax.rem(position + copies, sections), t)
-    swap_to = (h * copies + s, side * low + i)
+    home_peer = (position, side * low + i)
     mine_rel = jnp.where(home, 0, 1)
 
     def peer(d):
@@ -90,10 +90,6 @@
     for d in range(1, tensors):
         greet(peer(d))
 
-    @pl.when(away)
-    def _():
-        greet(swap_to)
-
     @pl.when(s > 0)
     def _():
         for u in range(tensors):
@@ -104,19 +100,22 @@
         for u in range(tensors):
             greet((position + 1, u))
 
-    greeted = tensors + jnp.where(away, 1, 0)
-    greeted += jnp.where(s > 0, tensors, 0) + jnp.where(s < copies - 1, tensors, 0)
+    greeted = tensors + jnp.where(s > 0, tensors, 0) + jnp.where(s < copies - 1, tensors, 0)
     pl.semaphore_wait(barrier, greeted)
 
     source = {X0: saved.at[0], X1: saved.at[1], G0: first}
     order = (X0, G0, X1)
 
+    def rows_of(way):
+        return pl.ds(way * rows, rows)
+
     for k in order:
-        for way, target in ((0, mirror), (1, swap_to)):
-            part_rows = pl.ds(way * rows, rows)
-            send(lambda k=k, way=way, target=target, part_rows=part_rows: remote(
-                source[k].at[part_rows, :], inb.at[k, 1, part_rows, cols(i)],
-                swp_s.at[k, way], swp_r.at[k], target), away)
+        send(lambda k=k: remote(
+            source[k].at[rows_of(0), :], inb.at[k, 1, rows_of(0), cols(i)],
+            swp_s.at[k], swp_r.at[k], mirror), away)
+        send(lambda k=k: remote(
+            source[k].at[rows_of(1), :], via.at[k],
+            via_s.at[k], via_r.at[k], home_peer), away)
     for k in order:
         for d in range(1, tensors):
             send(lambda k=k, d=d: remote(
@@ -126,6 +125,15 @@
         @pl.when(home)
         def _(k=k):
             pltpu.make_async_copy(source[k], inb.at[k, 0, :, cols(i)], loc_sem.at[k]).start()
+
+    for k in order:
+        @pl.when(home)
+        def _(k=k):
+            arrived(via.at[k], via_r.at[k])
+
+        send(lambda k=k: remote(
+            via.at[k], inb.at[k, 1, rows_of(1), cols(i)],
+            swp_s.at[k], swp_r.at[k], mirror), home)
 
     def head_copy(d, rel_slot):
         which = side if rel_slot == 0 else 1 - side
@@ -346,6 +354,7 @@
             pltpu.VMEM((half, inner), BF16),
             pltpu.VMEM((inner, half), BF16),
             pltpu.VMEM((4, 2, tok, half), BF16),
+            pltpu.VMEM((3, tok // 2, chunk), BF16),
             pltpu.VMEM((4, 2, tok, inner), BF16),
             pltpu.VMEM((4, 2, tok, inner), BF16),
             pltpu.VMEM((2, 2, tok, inner), BF16),
@@ -355,7 +364,7 @@
             pltpu.VMEM((2, tok, chunk), BF16),
             dma((2,)), dma((5,)), dma((9,)),
             dma((3, tensors - 1)), dma((3, low)),
-            dma((3, 2)), dma((3,)),
+            dma((3,)), dma((3,)), dma((3,)), dma((3,)),
             dma((3, tensors - 1)), dma((3, tensors - 1)),
             dma((4, 2)), dma((4, 2)),
             dma((2, 2, low)), dma((2, tensors - 1)),
@@ -363,7 +372,7 @@
             dma((2, tensors - 1)), dma((2, low)),
         ],
         compiler_params=pltpu.CompilerParams(
-            collective_id=0, has_side_effects=True, vmem_limit_bytes=48 * 2**20
+            collective_id=0, has_side_effects=True, vmem_limit_bytes=62 * 2**20
         ),
         cost_estimate=pl.CostEstimate(
             flops=24 * tok * half * inner, bytes_accessed=8 * half * inner, transcendentals=4 * tok * inner

time: 227 us -> 225 us (level)
    unnamed x9 -> x5, local copies, waits for them, and re-layouts: 3.46 us -> 0.66 us
  transfers between devices with their start and end apart: 1 -> 1, of which waited for: 0 -> 0; matrix products, arithmetic and copies ran while one was open for 4% -> 5% of each run, Pallas kernels for 0% -> 0%
where the time goes in v4:
time: 225 us
  Pallas kernels  212 us (94%)
  matrix products  9.27 us (4%)
    pallas_call x1, Pallas kernels, body(): pl.pallas_call(functools.partial(chain, sections, tensors), out_shape=(sh...  212 us
    dot_general x2, matrix products, dot(): lax.dot_general(left, right, (((left_dim,), (right_dim,)), ((), ())), pre...  9.27 us
  transfers between devices with their start and end apart: 1, of which 0 were waited for; matrix products, arithmetic and copies ran while one was open for 5% of the time, Pallas kernels for 0%

profile of v4, /device:TPU:0, one launch (start us, length us, event | category | flops | bytes accessed | tf_op | source)
XLA Modules:
  0.0 225.2 jit_solution(408933023843800088)
XLA Ops:
  0.6 211.8 %shard_map.76 = (bf16[2,2,128,1024]{3,2,1,0:T(8,128)(2,1)}, bf16[2,128,2048]{2,1,0:T(8,128)(2,1)}, bf16[2,128,2048]{2,1,0:T(8,128)(2,1)}, bf16[1024,2048]{1,0:T(...) custom-call(bf16[1024,2048]{1,0:T(8,128)(2,1)} %bitcast.20, bf16[2048,1024]{1,0:T(8,128)(2,1)} %bitcast.21, ...), custom_call_target="tpu_custom_call" | custom-call | flops 6442450944 | bytes 16777216 | tf_op jit(solution)/shard_map/pallas_call | solution.py:339
  212.5 1.6 collective-permute-start
  214.0 1.3 fusion.2
  215.3 0.0 copy-start
  215.3 0.0 copy-start.1
  215.3 6.0 %fusion.1 = bf16[1,2048,1024]{2,1,0:T(8,128)(2,1)} fusion(bf16[256,2048]{1,0:T(8,128)(2,1)} %bitcast.25, bf16[256,1024]{1,0:T(8,128)(2,1)S(1)} %bitcast.18, bf16[2048,1024]{1,0:T(8,128)(2,1)} %get-tuple-element.13), kind=kOutput, calls=%fused_computation.3 | convolution fusion | flops 1080033280 | bytes 9961472 | tf_op jit(solution)/shard_map/dot_general | solution.py:18
  221.3 0.0 copy-done
  221.3 0.0 copy-done.1
  221.3 3.3 %fusion = bf16[1,1024,2048]{2,1,0:T(8,128)(2,1)} fusion(bf16[256,1024]{1,0:T(8,128)(2,1)S(1)} %bitcast.17, bf16[256,2048]{1,0:T(8,128)(2,1)S(1)} %bitcast.24, bf16[1024,2048]{1,0:T(8,128)(2,1)S(1)} %copy-done.1), kind=kOutput, calls=%fused_computation.2 | convolution fusion | flops 1080033280 | bytes 9961472 | tf_op jit(solution)/shard_map/dot_general | solution.py:18
  224.6 0.0 collective-permute-done
  224.6 0.7 copy.9
Async XLA Ops:
  212.5 12.1 %collective-permute-start = (bf16[128,512]{1,0:T(8,128)(2,1)}, bf16[128,512]{1,0:T(8,128)(2,1)S(1)}, u32[]{:S(2)}, u32[]{:S(2)}) collective-permute-start(bf16[128,512]{1,0:T(8,128)(2,1)} %get-tuple-element.9), channel_id=1, source_target_pairs={{0,0},{1,1},{2,16},{3,17},{4,4},{5,5},{6,20},{7,21},{8,8},{9,9},{1... | collective-permute-start | bytes 393224 | tf_op jit(solution)/shard_map/ppermute | solution.py:387
  215.3 6.0 %copy-start = (bf16[2,128,2048]{2,1,0:T(8,128)(2,1)S(1)}, bf16[2,128,2048]{2,1,0:T(8,128)(2,1)}, u32[]{:S(2)}) copy-start(bf16[2,128,2048]{2,1,0:T(8,128)(2,1)} %get-tuple-element.12) | copy-start | bytes 3145732
  215.3 6.0 %copy-start.1 = (bf16[1024,2048]{1,0:T(8,128)(2,1)S(1)}, bf16[1024,2048]{1,0:T(8,128)(2,1)}, u32[]{:S(2)}) copy-start(bf16[1024,2048]{1,0:T(8,128)(2,1)} %get-tuple-element.10) | copy-start | bytes 12582916
